TPU v7x, 32 devices: a whole 2x2x4 slice. The times are simulated.
32 devices in a mesh: seq: 16 (over z, y, core), pair: 2 (over x).
Axes of the slice: x: 2, y: 2, z: 4, core: 2. Of those that a mesh axis runs over, the one named last changes fastest.
Arguments:
- student: float32 [10240, 1408], P('seq'), may hold values from -640 to 640
- teacher: float32 [10240, 1408], P('seq'), may hold values from -640 to 640
Outputs:
- student_grad: float32 [10240, 1408], P('seq')
All inputs are finite; a program needn't handle non-finite values.
Results may differ from a plain program's by a relative error of at most 0.0059.
Values may be sent and summed in bfloat16 or wider, within the bound.
No kernel may reach another device: no remote copies, remote signals or barrier semaphores. Data moves between devices by JAX's collectives and lax.ppermute only.
A program may use at most 64 MiB of HBM per device.

v0:
```python
import math

import jax
import jax.numpy as jnp
from jax import lax
from jax.sharding import PartitionSpec as P


def from_behind(block, axis, distance):
    devices = range(lax.axis_size(axis))
    route = [((i - distance) % len(devices), i) for i in devices]
    return lax.ppermute(block, axis, route)


def normalize(values, width):
    scale = lax.rsqrt(jnp.sum(values * values, axis=1, keepdims=True) + width * 1e-06)
    return (scale, values * scale)


def relation_tile(own_s, own_t, partner, margin, weight):
    contract = (((1,), (1,)), ((), ()))
    s_rel = lax.dot_general(own_s, partner[0], contract, preferred_element_type=jnp.float32)
    t_rel = lax.dot_general(own_t, partner[1], contract, preferred_element_type=jnp.float32)
    delta = s_rel - t_rel
    shrink = jnp.maximum(delta - margin, 0.0) + jnp.minimum(delta + margin, 0.0)
    relation = (weight * shrink).astype(jnp.bfloat16)
    return jnp.dot(relation, partner[0], preferred_element_type=jnp.float32)


def finish_rows(scale, unit, unit_grad):
    dotted = jnp.sum(unit * unit_grad, axis=1, keepdims=True)
    return scale * (unit_grad - unit * dotted)


def local(student, teacher):
    rows, width = student.shape
    seq_count = lax.axis_size("seq")
    pair_count = lax.axis_size("pair")
    block_count = seq_count // pair_count
    bit_count = pair_count.bit_length() - 1
    pair_index = lax.axis_index("pair")
    margin = 0.75 / math.sqrt(width)
    weight = 64.0 * width / math.sqrt(rows * seq_count)
    s_scale, s_unit = normalize(student, width)
    t_scale, t_unit = normalize(teacher, width)
    s_half = s_unit.astype(jnp.bfloat16)
    t_half = t_unit.astype(jnp.bfloat16)
    partner = jnp.stack([s_half, t_half])

    def tile(block):
        return relation_tile(s_half, t_half, block, margin, weight)

    for bit in range(bit_count):
        moved = from_behind(partner, "seq", 1 << bit)
        partner = jnp.where(pair_index // (1 << bit) % 2 == 1, moved, partner)

    def advance(step, carry):
        block, total = carry
        block = from_behind(block, "seq", pair_count)
        return (block, total + tile(block))

    partial_value = tile(partner)
    partner, partial_value = lax.fori_loop(0, block_count - 1, advance, (partner, partial_value))
    unit_grad = lax.psum(partial_value, "pair")
    return finish_rows(s_scale, s_unit, unit_grad)


def solution(mesh):
    placed = (P("seq", None), P("seq", None))
    return jax.shard_map(
        local, mesh=mesh, in_specs=placed, out_specs=P("seq", None), check_vma=False
    )
```

profile of v0, /device:TPU:0, one launch (start us, length us, event | category | flops | bytes accessed | tf_op | source)
XLA Modules:
  0.0 835.0 jit_solution(4033369516736616668)
XLA Ops:
  15.0 45.2 %collective-permute-done.1 = bf16[2,640,1408]{2,1,0:T(8,128)(2,1)} collective-permute-done((bf16[2,640,1408]{2,1,0:T(8,128)(2,1)}, bf16[2,640,1408]{2,1,0:T(8,128)(2,1)}, u32[]{:S(2)}, u32[]{:S(2)}) %collective-permute-start.1) | collective-permute-done | bytes 3604512 | tf_op jit(solution)/shard_map/ppermute | solution.py:12
  65.6 8.1 fusion.11
  73.7 653.9 %while.14 = (s32[]{:T(128)}, bf16[2,640,1408]{2,1,0:T(8,128)(2,1)}, f32[640,1408]{1,0:T(8,128)}, bf16[640,1408]{1,0:T(8,128)(2,1)}, bf16[640,1408]{1,0:T(8,128)(2,1)S(1)}, /*index=5*/s32[]{:T(128)}) while((s32[]{:T(128)}, bf16[2,640,1408]{2,1,0:T(8,128)(2,1)}, f32[640,1408]{1,0:T(8,128)}, bf16[640,1408]{1,0:T(8,128)(2,1)}, ...), condition=%wide.region_3.4_spmd, body=%wide.region_2.3_spmd.sunk | while | flops 3464478720 | bytes 41123948 | solution.py:63
  73.7 79.7 %collective-permute-done = bf16[2,640,1408]{2,1,0:T(8,128)(2,1)} collective-permute-done((bf16[2,640,1408]{2,1,0:T(8,128)(2,1)}, bf16[2,640,1408]{2,1,0:T(8,128)(2,1)}, u32[]{:S(2)}, u32[]{:S(2)}) %collective-permute-start) | collective-permute-done | bytes 3604512 | tf_op jit(solution)/shard_map/while/body/eval_jaxpr/ppermute | solution.py:12
  153.5 4.1 copy.10
  157.6 3.2 fusion.30
  160.8 9.2 %convolution_add_fusion.2 = f32[640,1408]{1,0:T(8,128)} fusion(f32[640,1408]{1,0:T(8,128)} %get-tuple-element.122, bf16[2,640,1408]{2,1,0:T(8,128)(2,1)} %collective-permute-done, f32[640,640]{1,0:T(8,128)S(1)} %fusion.30, bf16[640,1408]{1,0:T(8,128)(2,1)} %get-tuple-element.129), kind=kOutput, calls=%fused_computation.clone.1 | convolution fusion | flops 2311045120 | bytes 14254080 | tf_op jit(solution)/shard_map/while/body/eval_jaxpr/dot_general | solution.py:27
  169.9 78.8 %collective-permute-done = bf16[2,640,1408]{2,1,0:T(8,128)(2,1)} collective-permute-done((bf16[2,640,1408]{2,1,0:T(8,128)(2,1)}, bf16[2,640,1408]{2,1,0:T(8,128)(2,1)}, u32[]{:S(2)}, u32[]{:S(2)}) %collective-permute-start) | collective-permute-done | bytes 3604512 | tf_op jit(solution)/shard_map/while/body/eval_jaxpr/ppermute | solution.py:12
  248.8 4.1 copy.10
  252.9 3.2 fusion.30
  256.0 9.2 %convolution_add_fusion.2 = f32[640,1408]{1,0:T(8,128)} fusion(f32[640,1408]{1,0:T(8,128)} %get-tuple-element.122, bf16[2,640,1408]{2,1,0:T(8,128)(2,1)} %collective-permute-done, f32[640,640]{1,0:T(8,128)S(1)} %fusion.30, bf16[640,1408]{1,0:T(8,128)(2,1)} %get-tuple-element.129), kind=kOutput, calls=%fused_computation.clone.1 | convolution fusion | flops 2311045120 | bytes 14254080 | tf_op jit(solution)/shard_map/while/body/eval_jaxpr/dot_general | solution.py:27
  265.2 77.9 %collective-permute-done = bf16[2,640,1408]{2,1,0:T(8,128)(2,1)} collective-permute-done((bf16[2,640,1408]{2,1,0:T(8,128)(2,1)}, bf16[2,640,1408]{2,1,0:T(8,128)(2,1)}, u32[]{:S(2)}, u32[]{:S(2)}) %collective-permute-start) | collective-permute-done | bytes 3604512 | tf_op jit(solution)/shard_map/while/body/eval_jaxpr/ppermute | solution.py:12
  343.1 4.1 copy.10
  347.2 3.2 fusion.30
  350.4 9.2 %convolution_add_fusion.2 = f32[640,1408]{1,0:T(8,128)} fusion(f32[640,1408]{1,0:T(8,128)} %get-tuple-element.122, bf16[2,640,1408]{2,1,0:T(8,128)(2,1)} %collective-permute-done, f32[640,640]{1,0:T(8,128)S(1)} %fusion.30, bf16[640,1408]{1,0:T(8,128)(2,1)} %get-tuple-element.129), kind=kOutput, calls=%fused_computation.clone.1 | convolution fusion | flops 2311045120 | bytes 14254080 | tf_op jit(solution)/shard_map/while/body/eval_jaxpr/dot_general | solution.py:27
  359.5 77.0 %collective-permute-done = bf16[2,640,1408]{2,1,0:T(8,128)(2,1)} collective-permute-done((bf16[2,640,1408]{2,1,0:T(8,128)(2,1)}, bf16[2,640,1408]{2,1,0:T(8,128)(2,1)}, u32[]{:S(2)}, u32[]{:S(2)}) %collective-permute-start) | collective-permute-done | bytes 3604512 | tf_op jit(solution)/shard_map/while/body/eval_jaxpr/ppermute | solution.py:12
  436.5 4.1 copy.10
  443.8 9.2 %convolution_add_fusion.2 = f32[640,1408]{1,0:T(8,128)} fusion(f32[640,1408]{1,0:T(8,128)} %get-tuple-element.122, bf16[2,640,1408]{2,1,0:T(8,128)(2,1)} %collective-permute-done, f32[640,640]{1,0:T(8,128)S(1)} %fusion.30, bf16[640,1408]{1,0:T(8,128)(2,1)} %get-tuple-element.129), kind=kOutput, calls=%fused_computation.clone.1 | convolution fusion | flops 2311045120 | bytes 14254080 | tf_op jit(solution)/shard_map/while/body/eval_jaxpr/dot_general | solution.py:27
  452.9 76.0 %collective-permute-done = bf16[2,640,1408]{2,1,0:T(8,128)(2,1)} collective-permute-done((bf16[2,640,1408]{2,1,0:T(8,128)(2,1)}, bf16[2,640,1408]{2,1,0:T(8,128)(2,1)}, u32[]{:S(2)}, u32[]{:S(2)}) %collective-permute-start) | collective-permute-done | bytes 3604512 | tf_op jit(solution)/shard_map/while/body/eval_jaxpr/ppermute | solution.py:12
  529.0 4.1 copy.10
  533.1 3.2 fusion.30
  536.2 9.2 %convolution_add_fusion.2 = f32[640,1408]{1,0:T(8,128)} fusion(f32[640,1408]{1,0:T(8,128)} %get-tuple-element.122, bf16[2,640,1408]{2,1,0:T(8,128)(2,1)} %collective-permute-done, f32[640,640]{1,0:T(8,128)S(1)} %fusion.30, bf16[640,1408]{1,0:T(8,128)(2,1)} %get-tuple-element.129), kind=kOutput, calls=%fused_computation.clone.1 | convolution fusion | flops 2311045120 | bytes 14254080 | tf_op jit(solution)/shard_map/while/body/eval_jaxpr/dot_general | solution.py:27
  545.4 75.1 %collective-permute-done = bf16[2,640,1408]{2,1,0:T(8,128)(2,1)} collective-permute-done((bf16[2,640,1408]{2,1,0:T(8,128)(2,1)}, bf16[2,640,1408]{2,1,0:T(8,128)(2,1)}, u32[]{:S(2)}, u32[]{:S(2)}) %collective-permute-start) | collective-permute-done | bytes 3604512 | tf_op jit(solution)/shard_map/while/body/eval_jaxpr/ppermute | solution.py:12
  620.5 4.1 copy.10
  624.6 3.2 fusion.30
  627.8 9.2 %convolution_add_fusion.2 = f32[640,1408]{1,0:T(8,128)} fusion(f32[640,1408]{1,0:T(8,128)} %get-tuple-element.122, bf16[2,640,1408]{2,1,0:T(8,128)(2,1)} %collective-permute-done, f32[640,640]{1,0:T(8,128)S(1)} %fusion.30, bf16[640,1408]{1,0:T(8,128)(2,1)} %get-tuple-element.129), kind=kOutput, calls=%fused_computation.clone.1 | convolution fusion | flops 2311045120 | bytes 14254080 | tf_op jit(solution)/shard_map/while/body/eval_jaxpr/dot_general | solution.py:27
  637.0 74.2 %collective-permute-done = bf16[2,640,1408]{2,1,0:T(8,128)(2,1)} collective-permute-done((bf16[2,640,1408]{2,1,0:T(8,128)(2,1)}, bf16[2,640,1408]{2,1,0:T(8,128)(2,1)}, u32[]{:S(2)}, u32[]{:S(2)}) %collective-permute-start) | collective-permute-done | bytes 3604512 | tf_op jit(solution)/shard_map/while/body/eval_jaxpr/ppermute | solution.py:12
  711.2 4.1 copy.10
  715.3 3.2 fusion.30
  718.4 9.2 %convolution_add_fusion.2 = f32[640,1408]{1,0:T(8,128)} fusion(f32[640,1408]{1,0:T(8,128)} %get-tuple-element.122, bf16[2,640,1408]{2,1,0:T(8,128)(2,1)} %collective-permute-done, f32[640,640]{1,0:T(8,128)S(1)} %fusion.30, bf16[640,1408]{1,0:T(8,128)(2,1)} %get-tuple-element.129), kind=kOutput, calls=%fused_computation.clone.1 | convolution fusion | flops 2311045120 | bytes 14254080 | tf_op jit(solution)/shard_map/while/body/eval_jaxpr/dot_general | solution.py:27
  727.6 92.9 %all-reduce.2.cloned.1.call-done = f32[640,1408]{1,0:T(8,128)} async-done(((f32[640,1408]{1,0:T(8,128)}), f32[640,1408]{1,0:T(8,128)}) %all-reduce.2.cloned.1.call-update) | async-done | bytes 3604496 | tf_op jit(solution)/shard_map/psum | solution.py:64
  820.6 3.7 multiply_reduce_fusion
  (32 shorter events, 21.0 us)
Async XLA Ops:
  6.5 814.0 %all-reduce.2.cloned.1.call-start = ((), (), s32[]{:S(2)}) async-start(), calls=%async_computation | async-start | bytes 7208960 | tf_op jit(solution)/shard_map/psum | solution.py:64
  6.5 3.1 copy-start
  9.6 2.0 copy-start.3
  12.1 2.4 copy-start.2
  14.5 45.6 %collective-permute-start.1 = (bf16[2,640,1408]{2,1,0:T(8,128)(2,1)}, bf16[2,640,1408]{2,1,0:T(8,128)(2,1)}, u32[]{:S(2)}, u32[]{:S(2)}) collective-permute-start(bf16[2,640,1408]{2,1,0:T(8,128)(2,1)} %pad_maximum_fusion), channel_id=1, source_target_pairs={{30,0},{0,2},{2,4},{4,6},{6,8},{8,10},{10,12},{12,14},{14,16},{16,... | collective-permute-start | bytes 10813448 | tf_op jit(solution)/shard_map/ppermute | solution.py:12
  62.1 1.8 copy-start.5
  73.7 79.7 %collective-permute-start = (bf16[2,640,1408]{2,1,0:T(8,128)(2,1)}, bf16[2,640,1408]{2,1,0:T(8,128)(2,1)}, u32[]{:S(2)}, u32[]{:S(2)}) collective-permute-start(bf16[2,640,1408]{2,1,0:T(8,128)(2,1)} %get-tuple-element.121), channel_id=1, source_target_pairs={{28,0},{30,2},{0,4},{2,6},{4,8},{6,10},{8,12},{10,14},{12,16},{14,... | collective-permute-start | bytes 10813448 | tf_op jit(solution)/shard_map/while/body/eval_jaxpr/ppermute | solution.py:12
  169.9 78.8 %collective-permute-start = (bf16[2,640,1408]{2,1,0:T(8,128)(2,1)}, bf16[2,640,1408]{2,1,0:T(8,128)(2,1)}, u32[]{:S(2)}, u32[]{:S(2)}) collective-permute-start(bf16[2,640,1408]{2,1,0:T(8,128)(2,1)} %get-tuple-element.121), channel_id=1, source_target_pairs={{28,0},{30,2},{0,4},{2,6},{4,8},{6,10},{8,12},{10,14},{12,16},{14,... | collective-permute-start | bytes 10813448 | tf_op jit(solution)/shard_map/while/body/eval_jaxpr/ppermute | solution.py:12
  265.2 77.9 %collective-permute-start = (bf16[2,640,1408]{2,1,0:T(8,128)(2,1)}, bf16[2,640,1408]{2,1,0:T(8,128)(2,1)}, u32[]{:S(2)}, u32[]{:S(2)}) collective-permute-start(bf16[2,640,1408]{2,1,0:T(8,128)(2,1)} %get-tuple-element.121), channel_id=1, source_target_pairs={{28,0},{30,2},{0,4},{2,6},{4,8},{6,10},{8,12},{10,14},{12,16},{14,... | collective-permute-start | bytes 10813448 | tf_op jit(solution)/shard_map/while/body/eval_jaxpr/ppermute | solution.py:12
  359.5 77.0 %collective-permute-start = (bf16[2,640,1408]{2,1,0:T(8,128)(2,1)}, bf16[2,640,1408]{2,1,0:T(8,128)(2,1)}, u32[]{:S(2)}, u32[]{:S(2)}) collective-permute-start(bf16[2,640,1408]{2,1,0:T(8,128)(2,1)} %get-tuple-element.121), channel_id=1, source_target_pairs={{28,0},{30,2},{0,4},{2,6},{4,8},{6,10},{8,12},{10,14},{12,16},{14,... | collective-permute-start | bytes 10813448 | tf_op jit(solution)/shard_map/while/body/eval_jaxpr/ppermute | solution.py:12
  452.9 76.0 %collective-permute-start = (bf16[2,640,1408]{2,1,0:T(8,128)(2,1)}, bf16[2,640,1408]{2,1,0:T(8,128)(2,1)}, u32[]{:S(2)}, u32[]{:S(2)}) collective-permute-start(bf16[2,640,1408]{2,1,0:T(8,128)(2,1)} %get-tuple-element.121), channel_id=1, source_target_pairs={{28,0},{30,2},{0,4},{2,6},{4,8},{6,10},{8,12},{10,14},{12,16},{14,... | collective-permute-start | bytes 10813448 | tf_op jit(solution)/shard_map/while/body/eval_jaxpr/ppermute | solution.py:12
  545.4 75.1 %collective-permute-start = (bf16[2,640,1408]{2,1,0:T(8,128)(2,1)}, bf16[2,640,1408]{2,1,0:T(8,128)(2,1)}, u32[]{:S(2)}, u32[]{:S(2)}) collective-permute-start(bf16[2,640,1408]{2,1,0:T(8,128)(2,1)} %get-tuple-element.121), channel_id=1, source_target_pairs={{28,0},{30,2},{0,4},{2,6},{4,8},{6,10},{8,12},{10,14},{12,16},{14,... | collective-permute-start | bytes 10813448 | tf_op jit(solution)/shard_map/while/body/eval_jaxpr/ppermute | solution.py:12
  637.0 74.2 %collective-permute-start = (bf16[2,640,1408]{2,1,0:T(8,128)(2,1)}, bf16[2,640,1408]{2,1,0:T(8,128)(2,1)}, u32[]{:S(2)}, u32[]{:S(2)}) collective-permute-start(bf16[2,640,1408]{2,1,0:T(8,128)(2,1)} %get-tuple-element.121), channel_id=1, source_target_pairs={{28,0},{30,2},{0,4},{2,6},{4,8},{6,10},{8,12},{10,14},{12,16},{14,... | collective-permute-start | bytes 10813448 | tf_op jit(solution)/shard_map/while/body/eval_jaxpr/ppermute | solution.py:12
  820.5 4.1 copy-start.1
  820.6 5.2 copy-start.4
Sparse Core Ops, SparseCore 0:
  727.7 92.7 all-reduce.1
where the time goes:
time: 836 us; the launch traced here: 835 us
  waiting for transfers between devices  677 us (81%)
  matrix products  96.1 us (11%)
  local copies, waits for them, and re-layouts  34.3 us (4%)
  other arithmetic  13.7 us (2%)
  between operations  13.4 us (2%)
    ppermute x8, waiting for transfers between devices, from_behind(): return lax.ppermute(block, axis, route)  584 us
    psum x1, waiting for transfers between devices, local(): unit_grad = lax.psum(partial_value, 'pair')  92.9 us
    dot_general x8, matrix products, relation_tile(): return jnp.dot(relation, partner[0], preferred_element_type=jnp.float32)  72.2 us
    while x7, local copies, waits for them, and re-layouts  28.7 us
    dot_general x8, matrix products, relation_tile(): lax.dot_general(own_t, partner[1], contract, preferred_element_type=jnp.f...  23.9 us
  transfers between devices with their start and end apart: 9, of which 9 were waited for; matrix products, arithmetic and copies ran while one was open for 0% of the time, Pallas kernels for 0%

commit v1 on v0

v1 whole, which is shorter than its diff:
```python
import math

import jax
import jax.numpy as jnp
from jax import lax
from jax.sharding import PartitionSpec as P

CHUNKS = 2


def normalize(values, width):
    scale = lax.rsqrt(jnp.sum(values * values, axis=1, keepdims=True) + width * 1e-06)
    return (scale, values * scale)


def relation_tile(own_s, own_t, partner_s, partner_t, margin, weight):
    contract = (((1,), (1,)), ((), ()))
    s_rel = lax.dot_general(own_s, partner_s, contract, preferred_element_type=jnp.float32)
    t_rel = lax.dot_general(own_t, partner_t, contract, preferred_element_type=jnp.float32)
    delta = s_rel - t_rel
    shrink = jnp.maximum(delta - margin, 0.0) + jnp.minimum(delta + margin, 0.0)
    relation = (weight * shrink).astype(jnp.bfloat16)
    return jnp.dot(relation, partner_s, preferred_element_type=jnp.float32)


def project(unit, grad):
    return grad - unit * jnp.sum(unit * grad, axis=1, keepdims=True)


def sum_over_pair(value, count):
    distance = 1
    while distance < count:
        half = value.astype(jnp.bfloat16)
        other = lax.ppermute(half, "pair", [(i, i ^ distance) for i in range(count)])
        value = half.astype(jnp.float32) + other.astype(jnp.float32)
        distance *= 2
    return value


def local(student, teacher):
    rows, width = student.shape
    seq_count = lax.axis_size("seq")
    pair_count = lax.axis_size("pair")
    pair_index = lax.axis_index("pair")
    margin = 0.75 / math.sqrt(width)
    weight = 64.0 * width / math.sqrt(rows * seq_count)
    s_scale, s_unit = normalize(student, width)
    t_scale, t_unit = normalize(teacher, width)
    s_half = s_unit.astype(jnp.bfloat16)
    t_half = t_unit.astype(jnp.bfloat16)
    share = rows // pair_count
    piece = share // CHUNKS

    total = jnp.zeros((rows, width), jnp.float32)
    for chunk in range(CHUNKS):
        start = pair_index * share + chunk * piece
        s_part = lax.dynamic_slice_in_dim(s_half, start, piece, 0)
        t_part = lax.dynamic_slice_in_dim(t_half, start, piece, 0)
        all_s = lax.all_gather(s_part, "seq", axis=0, tiled=True)
        all_t = lax.all_gather(t_part, "seq", axis=0, tiled=True)
        total = total + relation_tile(s_half, t_half, all_s, all_t, margin, weight)
    return s_scale * sum_over_pair(project(s_unit, total), pair_count)


def solution(mesh):
    placed = (P("seq", None), P("seq", None))
    return jax.shard_map(
        local, mesh=mesh, in_specs=placed, out_specs=P("seq", None), check_vma=False
    )
```

time: 836 us -> 362 us (0.43)
  waiting for transfers between devices: 677 us -> 269 us
  matrix products: 96.1 us -> 62.2 us
  local copies, waits for them, and re-layouts: 34.3 us -> 4.56 us
    ppermute x8 -> x1, waiting for transfers between devices: 584 us -> 40 us  [sum_over_pair(): lax.ppermute(half, 'pair', [(i, i ^ distance) for i in range(count)])]
    all_gather x0 -> x4, waiting for transfers between devices: none -> 227 us  [the longest x2 121 us: local(): all_s = lax.all_gather(s_part, 'seq', axis=0, tiled=True)]
    psum x1 -> x0, waiting for transfers between devices: 92.9 us -> none  [local(): unit_grad = lax.psum(partial_value, 'pair')]
    dot_general x16 -> x4, matrix products: 96.1 us -> 62.2 us  [the longest x2 41.9 us: relation_tile(): return jnp.dot(relation, partner_s, preferred_element_type=jnp.float32)]
    while x7 -> x0, local copies, waits for them, and re-layouts: 28.7 us -> none
  transfers between devices with their start and end apart: 9 -> 5, of which waited for: 9 -> 5; matrix products, arithmetic and copies ran while one was open for 0% -> 12% of each run, Pallas kernels for 0% -> 0%
where the time goes in v1:
time: 362 us
  waiting for transfers between devices  269 us (74%)
  matrix products  62.2 us (17%)
  between operations  13.2 us (4%)
  other arithmetic  11.5 us (3%)
  local copies, waits for them, and re-layouts  4.56 us (1%)
    all_gather x2, waiting for transfers between devices, local(): all_s = lax.all_gather(s_part, 'seq', axis=0, tiled=True)  121 us
    all_gather x2, waiting for transfers between devices, local(): all_t = lax.all_gather(t_part, 'seq', axis=0, tiled=True)  106 us
    dot_general x2, matrix products, relation_tile(): return jnp.dot(relation, partner_s, preferred_element_type=jnp.float32)  41.9 us
    ppermute x1, waiting for transfers between devices, sum_over_pair(): lax.ppermute(half, 'pair', [(i, i ^ distance) for i in range(count)])  40 us
    dot_general x2, matrix products, relation_tile(): lax.dot_general(own_s, partner_s, contract, preferred_element_type=jnp.fl...  20.4 us
  transfers between devices with their start and end apart: 5, of which 5 were waited for; matrix products, arithmetic and copies ran while one was open for 12% of the time, Pallas kernels for 0%

profile of v1, /device:TPU:0, one launch (start us, length us, event | category | flops | bytes accessed | tf_op | source)
XLA Modules:
  0.0 361.7 jit_solution(9030448075970925972)
XLA Ops:
  6.5 0.0 all-gather.5.cloned.1.call-start
  6.5 2.5 multiply_reduce_fusion.2
  9.0 0.6 copy-done
  9.6 0.3 multiply_convert_fusion.3
  9.9 1.1 constant_dynamic-slice_fusion.1
  11.0 0.0 all-gather.5.cloned.1.call-update
  11.0 0.0 all-gather.9.cloned.1.call-start
  11.1 0.7 all-gather.9.cloned.1.call-update
  11.8 0.0 all-gather.7.cloned.1.call-start
  11.8 0.0 copy-start.1
  11.8 2.5 multiply_reduce_fusion.1
  14.3 0.6 copy-done.1
  14.9 0.3 multiply_convert_fusion.2
  15.2 0.0 copy-start.2
  15.2 1.2 copy-done.2
  16.4 1.0 constant_dynamic-slice_fusion
  17.5 0.0 all-gather.7.cloned.1.call-update
  17.5 0.0 all-gather.11.cloned.1.call-start
  17.5 0.5 all-gather.11.cloned.1.call-update
  18.1 63.2 %all-gather.5.cloned.1.call-done = bf16[2560,1408]{1,0:T(8,128)(2,1)} async-done(((bf16[160,1408]{1,0:T(8,128)(2,1)}), bf16[2560,1408]{1,0:T(8,128)(2,1)}) %all-gather.5.cloned.1.call-update) | async-done | bytes 7208976 | tf_op jit(solution)/shard_map/all_gather | solution.py:59
  81.3 10.2 %fusion.9 = f32[640,2560]{1,0:T(8,128)} fusion(bf16[640,1408]{1,0:T(8,128)(2,1)S(1)} %multiply_convert_fusion.3, bf16[2560,1408]{1,0:T(8,128)(2,1)} %all-gather.5.cloned.1.call-done), kind=kOutput, calls=%fused_computation.25 | convolution fusion | flops 4613734400 | bytes 15564800 | tf_op jit(solution)/shard_map/dot_general | solution.py:18
  91.5 58.0 %all-gather.9.cloned.1.call-done = bf16[2560,1408]{1,0:T(8,128)(2,1)} async-done(((bf16[160,1408]{1,0:T(8,128)(2,1)}), bf16[2560,1408]{1,0:T(8,128)(2,1)}) %all-gather.9.cloned.1.call-update) | async-done | bytes 7208976 | tf_op jit(solution)/shard_map/all_gather | solution.py:59
  149.5 10.2 %fusion.10 = f32[640,2560]{1,0:T(8,128)} fusion(bf16[640,1408]{1,0:T(8,128)(2,1)S(1)} %multiply_convert_fusion.3, bf16[2560,1408]{1,0:T(8,128)(2,1)} %all-gather.9.cloned.1.call-done), kind=kOutput, calls=%fused_computation.26 | convolution fusion | flops 4613734400 | bytes 15564800 | tf_op jit(solution)/shard_map/dot_general | solution.py:18
  159.7 58.0 %all-gather.7.cloned.1.call-done = bf16[2560,1408]{1,0:T(8,128)(2,1)} async-done(((bf16[160,1408]{1,0:T(8,128)(2,1)}), bf16[2560,1408]{1,0:T(8,128)(2,1)}) %all-gather.7.cloned.1.call-update) | async-done | bytes 7208976 | tf_op jit(solution)/shard_map/all_gather | solution.py:60
  217.7 20.0 %fusion = f32[640,1408]{1,0:T(8,128)} fusion(bf16[2560,1408]{1,0:T(8,128)(2,1)} %all-gather.5.cloned.1.call-done, f32[640,2560]{1,0:T(8,128)} %fusion.9, bf16[640,1408]{1,0:T(8,128)(2,1)} %copy-done.2, bf16[2560,1408]{1,0:T(8,128)(2,1)} %all-gather.7.cloned.1.call-done), kind=kOutput, calls=%fused_computation.10 | convolution fusion | flops 9240576000 | bytes 26378240 | tf_op jit(solution)/shard_map/dot_general | solution.py:23
  237.8 48.0 %all-gather.11.cloned.1.call-done = bf16[2560,1408]{1,0:T(8,128)(2,1)} async-done(((bf16[160,1408]{1,0:T(8,128)(2,1)}), bf16[2560,1408]{1,0:T(8,128)(2,1)}) %all-gather.11.cloned.1.call-update) | async-done | bytes 7208976 | tf_op jit(solution)/shard_map/all_gather | solution.py:60
  285.8 0.0 copy-done.3
  285.8 21.8 %multiply_reduce_fusion = (f32[640]{0:T(1024)S(1)}, f32[640,1408]{1,0:T(8,128)}) fusion(f32[640,1408]{1,0:T(8,128)} %param.2, f32[640]{0:T(1024)S(1)} %add_rsqrt_fusion.1, f32[640,1408]{1,0:T(8,128)} %fusion, bf16[2560,1408]{1,0:T(8,128)(2,1)} %all-gather.9.cloned.1.call-done, f32[640,2560]{1,0:T(8,128)} %fusion.10, bf16[640,1408]{1,0:T(8,128)(2,1)S(1)} %copy-done.3, ...), kind=kOutput, calls=%fused_computation.4 | convolution fusion | flops 9244179456 | bytes 33592320 | tf_op jit(solution)/shard_map/dot_general | solution.py:23
  307.6 3.6 %subtract_convert_fusion = bf16[640,1408]{1,0:T(8,128)(2,1)S(1)} fusion(f32[640,1408]{1,0:T(8,128)} %get-tuple-element.10, f32[640,1408]{1,0:T(8,128)} %param.2, f32[640]{0:T(1024)S(1)} %get-tuple-element.9, f32[640]{0:T(1024)S(1)} %add_rsqrt_fusion.1), kind=kLoop, calls=%fused_computation.3 | loop fusion | flops 3604480 | bytes 9016320 | tf_op jit(solution)/shard_map/convert_element_type | solution.py:33
  311.2 1.5 collective-permute-start
  312.8 40.0 %collective-permute-done = bf16[640,1408]{1,0:T(8,128)(2,1)S(1)} collective-permute-done((bf16[640,1408]{1,0:T(8,128)(2,1)S(1)}, bf16[640,1408]{1,0:T(8,128)(2,1)S(1)}, u32[]{:S(2)}, u32[]{:S(2)}) %collective-permute-start) | collective-permute-done | bytes 1802272 | tf_op jit(solution)/shard_map/ppermute | solution.py:34
  352.8 2.4 add_multiply_fusion
  (4 shorter events, 0.0 us)
Async XLA Ops:
  6.5 74.8 %all-gather.5.cloned.1.call-start = ((), (), s32[]{:S(2)}) async-start(), calls=%async_computation | async-start | bytes 7659520 | tf_op jit(solution)/shard_map/all_gather | solution.py:59
  6.5 3.1 copy-start
  11.0 138.5 %all-gather.9.cloned.1.call-start = ((), (), s32[]{:S(2)}) async-start(), calls=%async_computation.2 | async-start | bytes 7659520 | tf_op jit(solution)/shard_map/all_gather | solution.py:59
  11.8 206.0 %all-gather.7.cloned.1.call-start = ((), (), s32[]{:S(2)}) async-start(), calls=%async_computation.1 | async-start | bytes 7659520 | tf_op jit(solution)/shard_map/all_gather | solution.py:60
  11.8 3.1 copy-start.1
  15.2 1.2 copy-start.2
  17.5 268.3 %all-gather.11.cloned.1.call-start = ((), (), s32[]{:S(2)}) async-start(), calls=%async_computation.3 | async-start | bytes 7659520 | tf_op jit(solution)/shard_map/all_gather | solution.py:60
  159.7 126.1 %copy-start.3 = (bf16[640,1408]{1,0:T(8,128)(2,1)S(1)}, bf16[640,1408]{1,0:T(8,128)(2,1)}, u32[]{:S(2)}) copy-start(bf16[640,1408]{1,0:T(8,128)(2,1)} %copy-done.2) | copy-start | bytes 5406724
  311.2 41.5 %collective-permute-start = (bf16[640,1408]{1,0:T(8,128)(2,1)S(1)}, bf16[640,1408]{1,0:T(8,128)(2,1)S(1)}, u32[]{:S(2)}, u32[]{:S(2)}) collective-permute-start(bf16[640,1408]{1,0:T(8,128)(2,1)S(1)} %subtract_convert_fusion), channel_id=1, source_target_pairs={{0,1},{1,0},{2,3},{3,2},{4,5},{5,4},{6,7},{7,6},{8,9},{9,8},{10,11... | collective-permute-start | bytes 5406728 | tf_op jit(solution)/shard_map/ppermute | solution.py:34
Sparse Core Ops, SparseCore 0:
  11.1 70.1 all-gather.4
  83.6 65.8 all-gather.8
  151.8 65.8 all-gather.6
  219.9 65.8 all-gather.10
